TPU v7x, 256 devices: a whole 4x4x8 slice. The times are simulated.
256 devices in a mesh: rep: 8 (over z), shard: 32 (over x, y, core).
Axes of the slice: x: 4, y: 4, z: 8, core: 2. Of those that a mesh axis runs over, the one named last changes fastest.
Arguments:
- grads: bfloat16 [8, 8192, 8192], P('rep', 'shard'), may hold values from -40 to 40
- owner_table: int32 [32, 32, 1], P('shard'), may hold values from 0 to 31; in each aligned block of 32 rows (0 to 31, 32 to 63, ..., all dimensions but the last counted through in order) at most 2 rows name the same one
- left_roots: float32 [32, 32, 2, 256, 256], P('shard', 'rep'), may hold values from -1 to 2.5
- right_roots: float32 [32, 32, 2, 256, 256], P('shard', 'rep'), may hold values from -1 to 2.5
Outputs:
- direction: bfloat16 [8192, 8192], P('shard')
Inputs may be any that keep to these rules, and one draw needn't show every extreme that they name: `owner_table`: among the blocks of the rows of one index of shard (32 blocks), no owner is named more than 2 times, a bound that some block reaches.
All inputs are finite; a program needn't handle non-finite values.
Results may differ from a plain program's by a relative error of at most 0.019.
Values may be sent and summed in bfloat16 or wider, within the bound.
No kernel may reach another device: no remote copies, remote signals or barrier semaphores. Data moves between devices by JAX's collectives and lax.ppermute only.
A program may use at most 128 MiB of HBM per device.

v0:
```python
import functools

import jax
import jax.numpy as jnp
import numpy as np
from jax import lax
from jax.experimental import pallas as pl
from jax.experimental.pallas import tpu as pltpu
from jax.sharding import PartitionSpec as P

BS = 256
EPS = 1e-06
REPLICAS = 8
SIDE = 4
GROUPS = 2 * SIDE
VMEM_LIMIT = 32 * 1024 * 1024


def device(group, member):
    core, a, b = group // SIDE, group // 2 % 2, group % 2
    x = 2 * a + member // 2 + (2 if core and member // 2 == 0 else 0)
    y = 2 * b + member % 2 + (2 if core and member % 2 == 0 else 0)
    return (x % SIDE * SIDE + y % SIDE) * 2 + core


MEMBERS = [[device(g, j) for j in range(SIDE)] for g in range(GROUPS)]
PEERS = [[device(g, j) for g in range(GROUPS)] for j in range(SIDE)]

STEPS = {
    "same": (0, 0),
    "half": (4, 4),
    "up": (2, 2),
    "down": (-2, -2),
    "up_a": (1, 3),
    "up_b": (3, 1),
    "down_a": (-1, -3),
    "down_b": (-3, -1),
}
COLUMNS = [
    ["down", "same", "up_a", "up_b", "down_b", "down_a", "half", "up"],
    ["up_a", "up_b", "same", "up", "half", "down", "down_a", "down_b"],
    ["up_b", "up_a", "same", "up", "down_a", "down_b", "down", "half"],
    ["up", "half", "up_b", "down_a", "down", "same", "down_b", "up_a"],
]
REPLICA_AT = np.array(
    [
        [[(m + STEPS[name][m % 2]) % REPLICAS for m in range(REPLICAS)] for name in names]
        for names in COLUMNS
    ],
    dtype=np.int32,
)


def along_rep():
    return [
        (
            m * SIDE * GROUPS + device(g, j),
            int(REPLICA_AT[j, g, m]) * SIDE * GROUPS + device(g, j),
        )
        for m in range(REPLICAS)
        for g in range(GROUPS)
        for j in range(SIDE)
    ]


def aside():
    return [
        (
            int(REPLICA_AT[j, g, m]) * SIDE * GROUPS + SIDE * m + j,
            int(REPLICA_AT[j, g, m]) * SIDE * GROUPS + device(g, j),
        )
        for m in range(REPLICAS)
        for g in range(GROUPS)
        for j in range(SIDE)
    ]


def announce():
    return [
        (g * SIDE * GROUPS + SIDE * m + j, m * SIDE * GROUPS + device(g, j))
        for m in range(REPLICAS)
        for g in range(GROUPS)
        for j in range(SIDE)
    ]


def copy_all(copies):
    for copy in copies:
        copy.start()
    for copy in copies:
        copy.wait()


def place_kernel(index, wide, *rest):
    blocks, sems = rest[-2:]
    copy_all(
        [
            pltpu.make_async_copy(
                wide.at[:, pl.ds(c * BS, BS)], blocks.at[index[c]], sems.at[c]
            )
            for c in range(blocks.shape[0])
        ]
    )


def spread_kernel(index, blocks, wide, sems):
    copy_all(
        [
            pltpu.make_async_copy(
                blocks.at[index[c]], wide.at[:, pl.ds(c * BS, BS)], sems.at[c]
            )
            for c in range(blocks.shape[0])
        ]
    )


def pick_kernel(index, source, target, sems):
    copy_all(
        [
            pltpu.make_async_copy(source.at[index[n]], target.at[n], sems.at[n])
            for n in range(target.shape[0])
        ]
    )


def moved(kernel, index, operand, shapes, name, after=()):
    out = [jax.ShapeDtypeStruct(shape, operand.dtype) for shape in shapes]
    result = pl.pallas_call(
        kernel,
        out_shape=out,
        in_specs=[pl.BlockSpec(memory_space=pltpu.SMEM)]
        + [pl.BlockSpec(memory_space=pl.ANY)] * (1 + len(after)),
        out_specs=[pl.BlockSpec(memory_space=pl.ANY) for _ in out],
        scratch_shapes=[pltpu.SemaphoreType.DMA((len(out) * index.shape[0],))],
        compiler_params=pltpu.CompilerParams(vmem_limit_bytes=VMEM_LIMIT),
        name=name,
    )(index, operand, *after)
    return result if len(out) > 1 else result[0]


def pick(index, operand, name):
    return moved(pick_kernel, index, operand, [index.shape + operand.shape[1:]], name)


def pack_kernel(left, right, both):
    for n in range(left.shape[0]):
        both[n, 0] = left[n].astype(jnp.bfloat16)
        both[n, 1] = right[n].astype(jnp.bfloat16)


def pack(left, right):
    vmem = pl.BlockSpec(memory_space=pltpu.VMEM)
    return pl.pallas_call(
        pack_kernel,
        out_shape=jax.ShapeDtypeStruct((left.shape[0], 2, BS, BS), jnp.bfloat16),
        in_specs=[vmem] * 2,
        out_specs=vmem,
        compiler_params=pltpu.CompilerParams(vmem_limit_bytes=VMEM_LIMIT),
        name="pack",
    )(left, right)


def split(value):
    high = value.astype(jnp.bfloat16)
    return high, (value - high.astype(jnp.float32)).astype(jnp.bfloat16)


def precondition_kernel(inverse_count, totals, roots, result):
    dot = functools.partial(jnp.dot, preferred_element_type=jnp.float32)
    for n in range(totals.shape[0]):
        grad = (totals[n].astype(jnp.float32) * inverse_count).astype(jnp.bfloat16)
        left, right = roots[n, 0], roots[n, 1]
        high, low = split(dot(grad, right))
        precond = dot(left, high) + dot(left, low)
        wide = grad.astype(jnp.float32)
        scale = jnp.sqrt(jnp.mean(wide * wide) + EPS) / jnp.sqrt(
            jnp.mean(precond * precond) + EPS
        )
        result[n] = (precond * scale).astype(jnp.bfloat16)


def precondition(totals, roots, count):
    vmem = pl.BlockSpec(memory_space=pltpu.VMEM)
    return pl.pallas_call(
        functools.partial(precondition_kernel, 1.0 / count),
        out_shape=jax.ShapeDtypeStruct(totals.shape, jnp.bfloat16),
        in_specs=[vmem] * 2,
        out_specs=vmem,
        compiler_params=pltpu.CompilerParams(vmem_limit_bytes=VMEM_LIMIT),
        cost_estimate=pl.CostEstimate(
            flops=6 * totals.size * BS, bytes_accessed=8 * totals.size, transcendentals=0
        ),
        name="precondition",
    )(totals, roots)


def place_of(keys):
    order = jnp.arange(keys.shape[0], dtype=jnp.int32)
    before = (keys[None, :] < keys[:, None]) | (
        (keys[None, :] == keys[:, None]) & (order[None, :] < order[:, None])
    )
    return jnp.sum(before.astype(jnp.int32), axis=1)


def group_and_member(index):
    x, y, core = index // (2 * SIDE), index // 2 % SIDE, index % 2
    a, b = (x - core) % SIDE // 2, (y - core) % SIDE // 2
    return core * SIDE + a * 2 + b, x % 2 * 2 + y % 2


def key_of(owners):
    group, member = group_and_member(owners)
    return group * SIDE + member


def local(grads, owner_table, left_roots, right_roots):
    replicas = lax.axis_size("rep")
    everywhere = ("rep", "shard")
    width = grads.shape[2]
    count = width // BS
    capacity = left_roots.shape[2]
    slots = SIDE * capacity
    per_replica = count // replicas
    my_rep = lax.axis_index("rep")
    my_group, my_member = group_and_member(lax.axis_index("shard"))

    keys = key_of(owner_table.reshape(count))
    place = place_of(keys)
    stored = (place % replicas) * per_replica + place // replicas

    packed = pack(
        left_roots.reshape(slots, BS, BS), right_roots.reshape(slots, BS, BS)
    )
    roots = lax.all_to_all(
        packed.reshape(SIDE, capacity, 2, BS, BS),
        "shard",
        split_axis=0,
        concat_axis=0,
        axis_index_groups=MEMBERS,
        tiled=True,
    ).reshape(slots, 2, BS, BS)
    ordered = moved(place_kernel, stored, grads[0], [(count, BS, BS)], "place", (packed,))
    total = lax.psum_scatter(ordered, "rep", scatter_dimension=0, tiled=True)

    told = lax.ppermute(jnp.stack([keys, place]), everywhere, announce())
    sender_key, sender_place = told[0], told[1]
    serves = jnp.asarray(REPLICA_AT)[my_member, :, my_rep]
    slot_key = my_group * SIDE + jnp.arange(SIDE, dtype=jnp.int32)
    first = jnp.sum((sender_key[None, :] < slot_key[:, None]).astype(jnp.int32), axis=1)
    named = jnp.sum((sender_key[None, :] == slot_key[:, None]).astype(jnp.int32), axis=1)
    slot = jnp.arange(capacity, dtype=jnp.int32)
    slot_place = (first[:, None] + slot[None, :]).reshape(-1)
    slot_used = (slot[None, :] < named[:, None]).reshape(-1)
    taken = slot_used[None, :] & (slot_place[None, :] % replicas == serves[:, None])
    slot_order = jnp.arange(slots, dtype=jnp.int32)
    root_index = jnp.sum(jnp.where(taken, slot_order[None, :], 0), axis=1)

    held = serves[my_group] + replicas * jnp.arange(per_replica, dtype=jnp.int32)
    held_group = jnp.sum(
        jnp.where(sender_place[None, :] == held[:, None], sender_key[None, :], 0),
        axis=1,
    ) // SIDE

    roots = lax.all_to_all(
        pick(root_index, roots, "pick_roots"),
        "shard",
        split_axis=0,
        concat_axis=0,
        axis_index_groups=PEERS,
        tiled=True,
    )
    roots = pick(held_group, roots, "hold_roots")
    back = {b: a for a, b in aside()}
    roots = lax.ppermute(roots, everywhere, [(a, back[b]) for a, b in along_rep()])
    mine = precondition(total, roots, replicas)
    gathered = lax.all_gather(mine, "rep", axis=0, tiled=True)
    return moved(spread_kernel, stored, gathered, [(BS, width)], "spread")


def solution(mesh):
    placed = (
        P("rep", "shard", None),
        P("shard", None, None),
        P("shard", "rep", None, None, None),
        P("shard", "rep", None, None, None),
    )
    return jax.shard_map(
        local, mesh=mesh, in_specs=placed, out_specs=P("shard", None), check_vma=False
    )
```

profile of v0, /device:TPU:8, one launch (start us, length us, event | category | flops | bytes accessed | tf_op | source)
XLA Modules:
  0.0 180.3 jit_solution(10615504907865609364)
XLA Ops:
  6.5 0.7 fusion.5
  7.4 1.6 copy-done.4
  9.0 1.6 copy-done.5
  10.6 1.5 pack.1.rest_0_
  12.2 1.4 copy-done.2
  13.6 1.6 place.1
  15.1 2.0 %copy-done = bf16[32,256,256]{2,1,0:T(8,128)(2,1)} copy-done((bf16[32,256,256]{2,1,0:T(8,128)(2,1)}, bf16[32,256,256]{2,1,0:T(8,128)(2,1)S(1)}, u32[]{:S(2)}) %copy-start) | copy-done | bytes 4194328
  17.2 5.8 %all-to-all-start = ((bf16[4,2,2,256,256]{4,3,2,1,0:T(8,128)(2,1)}), bf16[4,2,2,256,256]{4,3,2,1,0:T(8,128)(2,1)S(1)}, u32[]{:S(2)}, u32[]{:S(2)}) async-start(bf16[4,2,2,256,256]{4,3,2,1,0:T(8,128)(2,1)} %bitcast.10), calls=%async_computation.1 | async-start | bytes 4194304 | tf_op jit(solution)/shard_map/all_to_all | solution.py:234
  23.0 3.4 %collective-permute-start = (s32[2,32]{1,0:T(2,128)S(1)}, s32[2,32]{1,0:T(2,128)S(1)}, u32[]{:S(2)}, u32[]{:S(2)}) collective-permute-start(s32[2,32]{1,0:T(2,128)S(1)} %pad_add_fusion), channel_id=1, source_target_pairs={{0,0},{1,2},{2,8},{3,10},{32,4},{33,6},{34,12},{35,14},{64,16},{65... | collective-permute-start | bytes 776 | tf_op jit(solution)/shard_map/ppermute | solution.py:245
  26.5 1.3 dynamic_slice.6
  28.5 0.7 dynamic-slice_bitcast_fusion
  29.2 6.5 %collective-permute-done = s32[2,32]{1,0:T(2,128)S(1)} collective-permute-done((s32[2,32]{1,0:T(2,128)S(1)}, s32[2,32]{1,0:T(2,128)S(1)}, u32[]{:S(2)}, u32[]{:S(2)}) %collective-permute-start) | collective-permute-done | bytes 288 | tf_op jit(solution)/shard_map/ppermute | solution.py:245
  36.4 1.0 all-to-all-done
  37.4 0.8 pick_roots.1
  38.2 1.3 copy-done.1
  39.6 4.6 %all-to-all-start.1 = ((bf16[8,2,256,256]{3,2,1,0:T(8,128)(2,1)}), bf16[8,2,256,256]{3,2,1,0:T(8,128)(2,1)S(1)}, u32[]{:S(2)}, u32[]{:S(2)}) async-start(bf16[8,2,256,256]{3,2,1,0:T(8,128)(2,1)} %copy-done.1), calls=%async_computation.2 | async-start | bytes 4194304 | tf_op jit(solution)/shard_map/all_to_all | solution.py:264
  44.2 26.8 %all-to-all-done.1.source = bf16[8,2,256,256]{3,2,1,0:T(8,128)(2,1)S(1)} async-done(((bf16[8,2,256,256]{3,2,1,0:T(8,128)(2,1)}), bf16[8,2,256,256]{3,2,1,0:T(8,128)(2,1)S(1)}, u32[]{:S(2)}, u32[]{:S(2)}) %all-to-all-start.1) | async-done | bytes 2097184 | tf_op jit(solution)/shard_map/all_to_all | solution.py:264
  71.6 6.7 %collective-permute-start.1 = (bf16[4,2,256,256]{3,2,1,0:T(8,128)(2,1)S(1)}, bf16[4,2,256,256]{3,2,1,0:T(8,128)(2,1)S(1)}, u32[]{:S(2)}, u32[]{:S(2)}) collective-permute-start(bf16[4,2,256,256]{3,2,1,0:T(8,128)(2,1)S(1)} %hold_roots.1), channel_id=1, source_target_pairs={{0,192},{2,33},{8,98},{10,67},{4,0},{6,97},{12,34},{14,131},{16,32... | collective-permute-start | bytes 3145736 | tf_op jit(solution)/shard_map/ppermute | solution.py:274
  78.3 17.0 %collective-permute-done.1.roots = bf16[4,2,256,256]{3,2,1,0:T(8,128)(2,1)S(1)} collective-permute-done((bf16[4,2,256,256]{3,2,1,0:T(8,128)(2,1)S(1)}, bf16[4,2,256,256]{3,2,1,0:T(8,128)(2,1)S(1)}, u32[]{:S(2)}, u32[]{:S(2)}) %collective-permute-start.1) | collective-permute-done | bytes 1048608 | tf_op jit(solution)/shard_map/ppermute | solution.py:274
  95.3 1.0 copy-done.6
  96.4 2.1 %precondition.1 = bf16[4,256,256]{2,1,0:T(8,128)(2,1)} custom-call(bf16[4,256,256]{2,1,0:T(8,128)(2,1)S(1)} %copy-done.6, bf16[4,2,256,256]{3,2,1,0:T(8,128)(2,1)S(1)} %collective-permute-done.1.roots), custom_call_target="tpu_custom_call" | custom-call | flops 402653184 | bytes 2097152 | tf_op jit(solution)/shard_map/precondition/pallas_call | solution.py:184
  98.5 70.0 %all-gather.2.cloned.1.call-done.blocks = bf16[32,256,256]{2,1,0:T(8,128)(2,1)} async-done(((bf16[4,256,256]{2,1,0:T(8,128)(2,1)}), bf16[32,256,256]{2,1,0:T(8,128)(2,1)}) %all-gather.2.cloned.1.call-update) | async-done | bytes 4194320 | tf_op jit(solution)/shard_map/all_gather | solution.py:276
  168.4 2.2 %copy-done.3 = bf16[32,256,256]{2,1,0:T(8,128)(2,1)S(1)} copy-done((bf16[32,256,256]{2,1,0:T(8,128)(2,1)S(1)}, bf16[32,256,256]{2,1,0:T(8,128)(2,1)}, u32[]{:S(2)}) %copy-start.3) | copy-done | bytes 4194328
  170.6 2.8 %spread.1 = bf16[256,8192]{1,0:T(8,128)(2,1)} custom-call(s32[32]{0:T(128)S(1)} %fusion.8.index, bf16[32,256,256]{2,1,0:T(8,128)(2,1)S(1)} %copy-done.3), custom_call_target="tpu_custom_call" | custom-call | tf_op jit(solution)/shard_map/spread/pallas_call | solution.py:128
  (29 shorter events, 2.4 us)
Async XLA Ops:
  6.5 88.8 %reduce-scatter.2.cloned.1.call-start = ((), (), s32[]{:S(2)}) async-start(), calls=%async_computation.3 | async-start | bytes 4718592 | tf_op jit(solution)/shard_map/reduce_scatter | solution.py:243
  7.4 1.6 copy-start.4
  9.0 1.6 copy-start.5
  10.6 2.9 %copy-start.2 = (bf16[1,256,8192]{2,1,0:T(8,128)(2,1)S(1)}, bf16[1,256,8192]{2,1,0:T(8,128)(2,1)}, u32[]{:S(2)}) copy-start(bf16[1,256,8192]{2,1,0:T(8,128)(2,1)} %param.5) | copy-start | bytes 12582916
  15.1 2.0 %copy-start = (bf16[32,256,256]{2,1,0:T(8,128)(2,1)}, bf16[32,256,256]{2,1,0:T(8,128)(2,1)S(1)}, u32[]{:S(2)}) copy-start(bf16[32,256,256]{2,1,0:T(8,128)(2,1)S(1)} %place.1) | copy-start | bytes 12582916
  17.2 5.8 %copy-start.7 = (s32[1,32,1]{1,2,0:T(1,128)S(1)}, s32[1,32,1]{1,2,0:T(1,128)}, u32[]{:S(2)}) copy-start(s32[1,32,1]{1,2,0:T(1,128)} %param.6) | copy-start | bytes 388
  17.2 20.3 %all-to-all-start = ((bf16[4,2,2,256,256]{4,3,2,1,0:T(8,128)(2,1)}), bf16[4,2,2,256,256]{4,3,2,1,0:T(8,128)(2,1)S(1)}, u32[]{:S(2)}, u32[]{:S(2)}) async-start(bf16[4,2,2,256,256]{4,3,2,1,0:T(8,128)(2,1)} %bitcast.10), calls=%async_computation.1 | async-start | bytes 4194304 | tf_op jit(solution)/shard_map/all_to_all | solution.py:234
  23.0 12.7 %collective-permute-start = (s32[2,32]{1,0:T(2,128)S(1)}, s32[2,32]{1,0:T(2,128)S(1)}, u32[]{:S(2)}, u32[]{:S(2)}) collective-permute-start(s32[2,32]{1,0:T(2,128)S(1)} %pad_add_fusion), channel_id=1, source_target_pairs={{0,0},{1,2},{2,8},{3,10},{32,4},{33,6},{34,12},{35,14},{64,16},{65... | collective-permute-start | bytes 776 | tf_op jit(solution)/shard_map/ppermute | solution.py:245
  38.2 1.3 copy-start.1
  39.6 31.4 %all-to-all-start.1 = ((bf16[8,2,256,256]{3,2,1,0:T(8,128)(2,1)}), bf16[8,2,256,256]{3,2,1,0:T(8,128)(2,1)S(1)}, u32[]{:S(2)}, u32[]{:S(2)}) async-start(bf16[8,2,256,256]{3,2,1,0:T(8,128)(2,1)} %copy-done.1), calls=%async_computation.2 | async-start | bytes 4194304 | tf_op jit(solution)/shard_map/all_to_all | solution.py:264
  44.2 124.3 %all-gather.2.cloned.1.call-start = ((), (), s32[]{:S(2)}) async-start(), calls=%async_computation.4 | async-start | bytes 4718592 | tf_op jit(solution)/shard_map/all_gather | solution.py:276
  71.6 23.7 %collective-permute-start.1 = (bf16[4,2,256,256]{3,2,1,0:T(8,128)(2,1)S(1)}, bf16[4,2,256,256]{3,2,1,0:T(8,128)(2,1)S(1)}, u32[]{:S(2)}, u32[]{:S(2)}) collective-permute-start(bf16[4,2,256,256]{3,2,1,0:T(8,128)(2,1)S(1)} %hold_roots.1), channel_id=1, source_target_pairs={{0,192},{2,33},{8,98},{10,67},{4,0},{6,97},{12,34},{14,131},{16,32... | collective-permute-start | bytes 3145736 | tf_op jit(solution)/shard_map/ppermute | solution.py:274
  95.3 1.0 copy-start.6
  168.4 2.2 %copy-start.3 = (bf16[32,256,256]{2,1,0:T(8,128)(2,1)S(1)}, bf16[32,256,256]{2,1,0:T(8,128)(2,1)}, u32[]{:S(2)}) copy-start(bf16[32,256,256]{2,1,0:T(8,128)(2,1)} %all-gather.2.cloned.1.call-done.blocks) | copy-start | bytes 12582916
Sparse Core Ops, SparseCore 0:
  17.3 58.1 reduce-scatter.1
  98.6 69.8 all-gather.1
where the time goes:
time: 182 us; the launch traced here: 180 us
  waiting for transfers between devices  121 us (66%)
  starting transfers between devices  20.4 us (11%)
  between operations  13.7 us (8%)
  local copies, waits for them, and re-layouts  13.4 us (7%)
  Pallas kernels  9.39 us (5%)
  other arithmetic  2.12 us (1%)
    all_gather x1, waiting for transfers between devices, local(): gathered = lax.all_gather(mine, 'rep', axis=0, tiled=True)  70 us
    all_to_all x1, waiting for transfers between devices, local(): lax.all_to_all(pick(root_index, roots, 'pick_roots'), 'shard', split_axis...  26.8 us
    ppermute x1, waiting for transfers between devices, local(): lax.ppermute(roots, everywhere, [(a, back[b]) for a, b in along_rep()])  17 us
    unnamed x16, local copies, waits for them, and re-layouts  11.2 us
    ppermute x1, starting transfers between devices, local(): lax.ppermute(roots, everywhere, [(a, back[b]) for a, b in along_rep()])  6.66 us
    ppermute x1, waiting for transfers between devices, local(): told = lax.ppermute(jnp.stack([keys, place]), everywhere, announce())  6.47 us
    pallas_call x4, Pallas kernels, moved(): pl.pallas_call(kernel, out_shape=out, in_specs=[pl.BlockSpec(memory_space...  5.8 us
    all_to_all x1, starting transfers between devices, local(): lax.all_to_all(packed.reshape(SIDE, capacity, 2, BS, BS), 'shard', split_...  5.77 us
  transfers between devices with their start and end apart: 6, of which 5 were waited for; matrix products, arithmetic and copies ran while one was open for 2% of the time, Pallas kernels for 1%

commit v1 on v0

--- a/solution.py
+++ b/solution.py
@@ -37,9 +37,9 @@
     "down_b": (-3, -1),
 }
 COLUMNS = [
-    ["down", "same", "up_a", "up_b", "down_b", "down_a", "half", "up"],
-    ["up_a", "up_b", "same", "up", "half", "down", "down_a", "down_b"],
-    ["up_b", "up_a", "same", "up", "down_a", "down_b", "down", "half"],
+    ["up", "same", "up_b", "up_a", "down_a", "down_b", "half", "down"],
+    ["same", "up", "up_a", "up_b", "down_a", "down_b", "half", "down"],
+    ["same", "up", "down_a", "up_b", "down", "half", "down_b", "up_a"],
     ["up", "half", "up_b", "down_a", "down", "same", "down_b", "up_a"],
 ]
 REPLICA_AT = np.array(

time: 182 us -> 180 us (0.989)
    all_gather x1, waiting for transfers between devices: 70 us -> 63.4 us  [local(): gathered = lax.all_gather(mine, 'rep', axis=0, tiled=True)]
    ppermute x1, waiting for transfers between devices: 17 us -> 23.5 us  [local(): lax.ppermute(roots, everywhere, [(a, back[b]) for a, b in along_rep()])]
where the time goes in v1:
time: 180 us; the launch traced here: 179 us
  waiting for transfers between devices  121 us (67%)
  starting transfers between devices  19.1 us (11%)
  between operations  13.7 us (8%)
  local copies, waits for them, and re-layouts  13.4 us (7%)
  Pallas kernels  9.39 us (5%)
  other arithmetic  2.12 us (1%)
    all_gather x1, waiting for transfers between devices, local(): gathered = lax.all_gather(mine, 'rep', axis=0, tiled=True)  63.4 us
    all_to_all x1, waiting for transfers between devices, local(): lax.all_to_all(pick(root_index, roots, 'pick_roots'), 'shard', split_axis...  26.8 us
    ppermute x1, waiting for transfers between devices, local(): lax.ppermute(roots, everywhere, [(a, back[b]) for a, b in along_rep()])  23.5 us
    unnamed x16, local copies, waits for them, and re-layouts  11.2 us
    ppermute x1, waiting for transfers between devices, local(): told = lax.ppermute(jnp.stack([keys, place]), everywhere, announce())  6.47 us
    pallas_call x4, Pallas kernels, moved(): pl.pallas_call(kernel, out_shape=out, in_specs=[pl.BlockSpec(memory_space...  5.8 us
    all_to_all x1, starting transfers between devices, local(): lax.all_to_all(packed.reshape(SIDE, capacity, 2, BS, BS), 'shard', split_...  5.77 us
    ppermute x1, starting transfers between devices, local(): lax.ppermute(roots, everywhere, [(a, back[b]) for a, b in along_rep()])  5.29 us
  transfers between devices with their start and end apart: 6, of which 5 were waited for; matrix products, arithmetic and copies ran while one was open for 2% of the time, Pallas kernels for 1%

profile of v1, /device:TPU:8, one launch (start us, length us, event | category | flops | bytes accessed | tf_op | source)
XLA Modules:
  0.0 178.8 jit_solution(15665516014992772761)
XLA Ops:
  6.5 0.7 fusion.5
  7.4 1.6 copy-done.4
  9.0 1.6 copy-done.5
  10.6 1.5 pack.1.rest_0_
  12.2 1.4 copy-done.2
  13.6 1.6 place.1
  15.1 2.0 %copy-done = bf16[32,256,256]{2,1,0:T(8,128)(2,1)} copy-done((bf16[32,256,256]{2,1,0:T(8,128)(2,1)}, bf16[32,256,256]{2,1,0:T(8,128)(2,1)S(1)}, u32[]{:S(2)}) %copy-start) | copy-done | bytes 4194328
  17.2 5.8 %all-to-all-start = ((bf16[4,2,2,256,256]{4,3,2,1,0:T(8,128)(2,1)}), bf16[4,2,2,256,256]{4,3,2,1,0:T(8,128)(2,1)S(1)}, u32[]{:S(2)}, u32[]{:S(2)}) async-start(bf16[4,2,2,256,256]{4,3,2,1,0:T(8,128)(2,1)} %bitcast.10), calls=%async_computation.1 | async-start | bytes 4194304 | tf_op jit(solution)/shard_map/all_to_all | solution.py:234
  23.0 3.4 %collective-permute-start = (s32[2,32]{1,0:T(2,128)S(1)}, s32[2,32]{1,0:T(2,128)S(1)}, u32[]{:S(2)}, u32[]{:S(2)}) collective-permute-start(s32[2,32]{1,0:T(2,128)S(1)} %pad_add_fusion), channel_id=1, source_target_pairs={{0,0},{1,2},{2,8},{3,10},{32,4},{33,6},{34,12},{35,14},{64,16},{65... | collective-permute-start | bytes 776 | tf_op jit(solution)/shard_map/ppermute | solution.py:245
  26.5 1.3 dynamic_slice.6
  28.5 0.7 dynamic-slice_bitcast_fusion
  29.2 6.5 %collective-permute-done = s32[2,32]{1,0:T(2,128)S(1)} collective-permute-done((s32[2,32]{1,0:T(2,128)S(1)}, s32[2,32]{1,0:T(2,128)S(1)}, u32[]{:S(2)}, u32[]{:S(2)}) %collective-permute-start) | collective-permute-done | bytes 288 | tf_op jit(solution)/shard_map/ppermute | solution.py:245
  36.4 1.0 all-to-all-done
  37.4 0.8 pick_roots.1
  38.2 1.3 copy-done.1
  39.6 4.6 %all-to-all-start.1 = ((bf16[8,2,256,256]{3,2,1,0:T(8,128)(2,1)}), bf16[8,2,256,256]{3,2,1,0:T(8,128)(2,1)S(1)}, u32[]{:S(2)}, u32[]{:S(2)}) async-start(bf16[8,2,256,256]{3,2,1,0:T(8,128)(2,1)} %copy-done.1), calls=%async_computation.2 | async-start | bytes 4194304 | tf_op jit(solution)/shard_map/all_to_all | solution.py:264
  44.2 26.8 %all-to-all-done.1.source = bf16[8,2,256,256]{3,2,1,0:T(8,128)(2,1)S(1)} async-done(((bf16[8,2,256,256]{3,2,1,0:T(8,128)(2,1)}), bf16[8,2,256,256]{3,2,1,0:T(8,128)(2,1)S(1)}, u32[]{:S(2)}, u32[]{:S(2)}) %all-to-all-start.1) | async-done | bytes 2097184 | tf_op jit(solution)/shard_map/all_to_all | solution.py:264
  71.6 5.3 %collective-permute-start.1 = (bf16[4,2,256,256]{3,2,1,0:T(8,128)(2,1)S(1)}, bf16[4,2,256,256]{3,2,1,0:T(8,128)(2,1)S(1)}, u32[]{:S(2)}, u32[]{:S(2)}) collective-permute-start(bf16[4,2,256,256]{3,2,1,0:T(8,128)(2,1)S(1)} %hold_roots.1), channel_id=1, source_target_pairs={{0,64},{2,1},{8,2},{10,67},{4,0},{6,65},{12,66},{14,131},{16,96},{... | collective-permute-start | bytes 3145736 | tf_op jit(solution)/shard_map/ppermute | solution.py:274
  76.9 23.5 %collective-permute-done.1.roots = bf16[4,2,256,256]{3,2,1,0:T(8,128)(2,1)S(1)} collective-permute-done((bf16[4,2,256,256]{3,2,1,0:T(8,128)(2,1)S(1)}, bf16[4,2,256,256]{3,2,1,0:T(8,128)(2,1)S(1)}, u32[]{:S(2)}, u32[]{:S(2)}) %collective-permute-start.1) | collective-permute-done | bytes 1048608 | tf_op jit(solution)/shard_map/ppermute | solution.py:274
  100.5 1.0 copy-done.6
  101.5 2.1 %precondition.1 = bf16[4,256,256]{2,1,0:T(8,128)(2,1)} custom-call(bf16[4,256,256]{2,1,0:T(8,128)(2,1)S(1)} %copy-done.6, bf16[4,2,256,256]{3,2,1,0:T(8,128)(2,1)S(1)} %collective-permute-done.1.roots), custom_call_target="tpu_custom_call" | custom-call | flops 402653184 | bytes 2097152 | tf_op jit(solution)/shard_map/precondition/pallas_call | solution.py:184
  103.6 63.4 %all-gather.2.cloned.1.call-done.blocks = bf16[32,256,256]{2,1,0:T(8,128)(2,1)} async-done(((bf16[4,256,256]{2,1,0:T(8,128)(2,1)}), bf16[32,256,256]{2,1,0:T(8,128)(2,1)}) %all-gather.2.cloned.1.call-update) | async-done | bytes 4194320 | tf_op jit(solution)/shard_map/all_gather | solution.py:276
  167.0 2.2 %copy-done.3 = bf16[32,256,256]{2,1,0:T(8,128)(2,1)S(1)} copy-done((bf16[32,256,256]{2,1,0:T(8,128)(2,1)S(1)}, bf16[32,256,256]{2,1,0:T(8,128)(2,1)}, u32[]{:S(2)}) %copy-start.3) | copy-done | bytes 4194328
  169.2 2.8 %spread.1 = bf16[256,8192]{1,0:T(8,128)(2,1)} custom-call(s32[32]{0:T(128)S(1)} %fusion.8.index, bf16[32,256,256]{2,1,0:T(8,128)(2,1)S(1)} %copy-done.3), custom_call_target="tpu_custom_call" | custom-call | tf_op jit(solution)/shard_map/spread/pallas_call | solution.py:128
  (29 shorter events, 2.4 us)
Async XLA Ops:
  6.5 93.9 %reduce-scatter.2.cloned.1.call-start = ((), (), s32[]{:S(2)}) async-start(), calls=%async_computation.3 | async-start | bytes 4718592 | tf_op jit(solution)/shard_map/reduce_scatter | solution.py:243
  7.4 1.6 copy-start.4
  9.0 1.6 copy-start.5
  10.6 2.9 %copy-start.2 = (bf16[1,256,8192]{2,1,0:T(8,128)(2,1)S(1)}, bf16[1,256,8192]{2,1,0:T(8,128)(2,1)}, u32[]{:S(2)}) copy-start(bf16[1,256,8192]{2,1,0:T(8,128)(2,1)} %param.5) | copy-start | bytes 12582916
  15.1 2.0 %copy-start = (bf16[32,256,256]{2,1,0:T(8,128)(2,1)}, bf16[32,256,256]{2,1,0:T(8,128)(2,1)S(1)}, u32[]{:S(2)}) copy-start(bf16[32,256,256]{2,1,0:T(8,128)(2,1)S(1)} %place.1) | copy-start | bytes 12582916
  17.2 5.8 %copy-start.7 = (s32[1,32,1]{1,2,0:T(1,128)S(1)}, s32[1,32,1]{1,2,0:T(1,128)}, u32[]{:S(2)}) copy-start(s32[1,32,1]{1,2,0:T(1,128)} %param.6) | copy-start | bytes 388
  17.2 20.3 %all-to-all-start = ((bf16[4,2,2,256,256]{4,3,2,1,0:T(8,128)(2,1)}), bf16[4,2,2,256,256]{4,3,2,1,0:T(8,128)(2,1)S(1)}, u32[]{:S(2)}, u32[]{:S(2)}) async-start(bf16[4,2,2,256,256]{4,3,2,1,0:T(8,128)(2,1)} %bitcast.10), calls=%async_computation.1 | async-start | bytes 4194304 | tf_op jit(solution)/shard_map/all_to_all | solution.py:234
  23.0 12.7 %collective-permute-start = (s32[2,32]{1,0:T(2,128)S(1)}, s32[2,32]{1,0:T(2,128)S(1)}, u32[]{:S(2)}, u32[]{:S(2)}) collective-permute-start(s32[2,32]{1,0:T(2,128)S(1)} %pad_add_fusion), channel_id=1, source_target_pairs={{0,0},{1,2},{2,8},{3,10},{32,4},{33,6},{34,12},{35,14},{64,16},{65... | collective-permute-start | bytes 776 | tf_op jit(solution)/shard_map/ppermute | solution.py:245
  38.2 1.3 copy-start.1
  39.6 31.4 %all-to-all-start.1 = ((bf16[8,2,256,256]{3,2,1,0:T(8,128)(2,1)}), bf16[8,2,256,256]{3,2,1,0:T(8,128)(2,1)S(1)}, u32[]{:S(2)}, u32[]{:S(2)}) async-start(bf16[8,2,256,256]{3,2,1,0:T(8,128)(2,1)} %copy-done.1), calls=%async_computation.2 | async-start | bytes 4194304 | tf_op jit(solution)/shard_map/all_to_all | solution.py:264
  44.2 122.8 %all-gather.2.cloned.1.call-start = ((), (), s32[]{:S(2)}) async-start(), calls=%async_computation.4 | async-start | bytes 4718592 | tf_op jit(solution)/shard_map/all_gather | solution.py:276
  71.6 28.8 %collective-permute-start.1 = (bf16[4,2,256,256]{3,2,1,0:T(8,128)(2,1)S(1)}, bf16[4,2,256,256]{3,2,1,0:T(8,128)(2,1)S(1)}, u32[]{:S(2)}, u32[]{:S(2)}) collective-permute-start(bf16[4,2,256,256]{3,2,1,0:T(8,128)(2,1)S(1)} %hold_roots.1), channel_id=1, source_target_pairs={{0,64},{2,1},{8,2},{10,67},{4,0},{6,65},{12,66},{14,131},{16,96},{... | collective-permute-start | bytes 3145736 | tf_op jit(solution)/shard_map/ppermute | solution.py:274
  100.5 1.0 copy-start.6
  167.0 2.2 %copy-start.3 = (bf16[32,256,256]{2,1,0:T(8,128)(2,1)S(1)}, bf16[32,256,256]{2,1,0:T(8,128)(2,1)}, u32[]{:S(2)}) copy-start(bf16[32,256,256]{2,1,0:T(8,128)(2,1)} %all-gather.2.cloned.1.call-done.blocks) | copy-start | bytes 12582916
Sparse Core Ops, SparseCore 0:
  17.3 58.1 reduce-scatter.1
  103.7 63.2 all-gather.1

commit v2 on v1

--- a/solution.py
+++ b/solution.py
@@ -165,33 +165,55 @@
     return high, (value - high.astype(jnp.float32)).astype(jnp.bfloat16)
 
 
-def precondition_kernel(inverse_count, totals, roots, result):
-    dot = functools.partial(jnp.dot, preferred_element_type=jnp.float32)
+def prepare_kernel(inverse_count, totals, means, sizes):
     for n in range(totals.shape[0]):
-        grad = (totals[n].astype(jnp.float32) * inverse_count).astype(jnp.bfloat16)
-        left, right = roots[n, 0], roots[n, 1]
-        high, low = split(dot(grad, right))
-        precond = dot(left, high) + dot(left, low)
-        wide = grad.astype(jnp.float32)
-        scale = jnp.sqrt(jnp.mean(wide * wide) + EPS) / jnp.sqrt(
-            jnp.mean(precond * precond) + EPS
-        )
-        result[n] = (precond * scale).astype(jnp.bfloat16)
-
-
-def precondition(totals, roots, count):
+        mean = (totals[n].astype(jnp.float32) * inverse_count).astype(jnp.bfloat16)
+        wide = mean.astype(jnp.float32)
+        means[n] = mean
+        sizes[n] = jnp.sqrt(jnp.mean(wide * wide) + EPS)
+
+
+def prepare(totals, count):
     vmem = pl.BlockSpec(memory_space=pltpu.VMEM)
     return pl.pallas_call(
-        functools.partial(precondition_kernel, 1.0 / count),
-        out_shape=jax.ShapeDtypeStruct(totals.shape, jnp.bfloat16),
-        in_specs=[vmem] * 2,
+        functools.partial(prepare_kernel, 1.0 / count),
+        out_shape=[
+            jax.ShapeDtypeStruct(totals.shape, jnp.bfloat16),
+            jax.ShapeDtypeStruct(totals.shape[:1], jnp.float32),
+        ],
+        in_specs=[vmem],
+        out_specs=[vmem, pl.BlockSpec(memory_space=pltpu.SMEM)],
+        compiler_params=pltpu.CompilerParams(vmem_limit_bytes=VMEM_LIMIT),
+        cost_estimate=pl.CostEstimate(
+            flops=64 * totals.size, bytes_accessed=8 * totals.size, transcendentals=0
+        ),
+        name="prepare",
+    )(totals)
+
+
+def precondition_kernel(sizes, means, roots, result):
+    dot = functools.partial(jnp.dot, preferred_element_type=jnp.float32)
+    for n in range(means.shape[0]):
+        left, right = roots[n, 0], roots[n, 1]
+        high, low = split(dot(means[n], right))
+        precond = dot(left, high) + dot(left, low)
+        scale = sizes[n] / jnp.sqrt(jnp.mean(precond * precond) + EPS)
+        result[n] = (precond * scale).astype(jnp.bfloat16)
+
+
+def precondition(means, sizes, roots):
+    vmem = pl.BlockSpec(memory_space=pltpu.VMEM)
+    return pl.pallas_call(
+        precondition_kernel,
+        out_shape=jax.ShapeDtypeStruct(means.shape, jnp.bfloat16),
+        in_specs=[pl.BlockSpec(memory_space=pltpu.SMEM), vmem, vmem],
         out_specs=vmem,
         compiler_params=pltpu.CompilerParams(vmem_limit_bytes=VMEM_LIMIT),
         cost_estimate=pl.CostEstimate(
-            flops=6 * totals.size * BS, bytes_accessed=8 * totals.size, transcendentals=0
+            flops=6 * means.size * BS, bytes_accessed=8 * means.size, transcendentals=0
         ),
         name="precondition",
-    )(totals, roots)
+    )(sizes, means, roots)
 
 
 def place_of(keys):
@@ -272,7 +294,8 @@
     roots = pick(held_group, roots, "hold_roots")
     back = {b: a for a, b in aside()}
     roots = lax.ppermute(roots, everywhere, [(a, back[b]) for a, b in along_rep()])
-    mine = precondition(total, roots, replicas)
+    means, sizes = prepare(total, replicas)
+    mine = precondition(means, sizes, roots)
     gathered = lax.all_gather(mine, "rep", axis=0, tiled=True)
     return moved(spread_kernel, stored, gathered, [(BS, width)], "spread")
 

time: 180 us -> 181 us (level)
  Pallas kernels: 9.39 us -> 11.8 us
  waiting for transfers between devices: 121 us -> 119 us
  transfers between devices with their start and end apart: 6 -> 6, of which waited for: 5 -> 5; matrix products, arithmetic and copies ran while one was open for 2% -> 2% of each run, Pallas kernels for 1% -> 2%
where the time goes in v2:
time: 181 us; the launch traced here: 179 us
  waiting for transfers between devices  119 us (66%)
  starting transfers between devices  19.1 us (11%)
  between operations  13.7 us (8%)
  local copies, waits for them, and re-layouts  13.4 us (7%)
  Pallas kernels  11.8 us (7%)
  other arithmetic  2.18 us (1%)
    all_gather x1, waiting for transfers between devices, local(): gathered = lax.all_gather(mine, 'rep', axis=0, tiled=True)  63.3 us
    all_to_all x1, waiting for transfers between devices, local(): lax.all_to_all(pick(root_index, roots, 'pick_roots'), 'shard', split_axis...  26.8 us
    ppermute x1, waiting for transfers between devices, local(): lax.ppermute(roots, everywhere, [(a, back[b]) for a, b in along_rep()])  21.8 us
    unnamed x16, local copies, waits for them, and re-layouts  11.1 us
    pallas_call x4, Pallas kernels, moved(): pl.pallas_call(kernel, out_shape=out, in_specs=[pl.BlockSpec(memory_space...  6.69 us
    ppermute x1, waiting for transfers between devices, local(): told = lax.ppermute(jnp.stack([keys, place]), everywhere, announce())  6.4 us
    all_to_all x1, starting transfers between devices, local(): lax.all_to_all(packed.reshape(SIDE, capacity, 2, BS, BS), 'shard', split_...  5.77 us
    ppermute x1, starting transfers between devices, local(): lax.ppermute(roots, everywhere, [(a, back[b]) for a, b in along_rep()])  5.29 us
  transfers between devices with their start and end apart: 6, of which 5 were waited for; matrix products, arithmetic and copies ran while one was open for 2% of the time, Pallas kernels for 2%

profile of v2, /device:TPU:8, one launch (start us, length us, event | category | flops | bytes accessed | tf_op | source)
XLA Modules:
  0.0 179.4 jit_solution(17613748447609382807)
XLA Ops:
  7.4 1.6 copy-done.4
  9.0 1.6 copy-done.5
  10.6 1.6 pack.1.rest_0_
  12.2 1.4 copy-done.2
  13.6 1.6 place.1
  15.1 2.0 %copy-done = bf16[32,256,256]{2,1,0:T(8,128)(2,1)} copy-done((bf16[32,256,256]{2,1,0:T(8,128)(2,1)}, bf16[32,256,256]{2,1,0:T(8,128)(2,1)S(1)}, u32[]{:S(2)}) %copy-start) | copy-done | bytes 4194328
  17.2 5.8 %all-to-all-start = ((bf16[4,2,2,256,256]{4,3,2,1,0:T(8,128)(2,1)}), bf16[4,2,2,256,256]{4,3,2,1,0:T(8,128)(2,1)S(1)}, u32[]{:S(2)}, u32[]{:S(2)}) async-start(bf16[4,2,2,256,256]{4,3,2,1,0:T(8,128)(2,1)} %bitcast.10), calls=%async_computation.1 | async-start | bytes 4194304 | tf_op jit(solution)/shard_map/all_to_all | solution.py:256
  23.0 3.4 %collective-permute-start = (s32[2,32]{1,0:T(2,128)S(1)}, s32[2,32]{1,0:T(2,128)S(1)}, u32[]{:S(2)}, u32[]{:S(2)}) collective-permute-start(s32[2,32]{1,0:T(2,128)S(1)} %pad_add_fusion), channel_id=1, source_target_pairs={{0,0},{1,2},{2,8},{3,10},{32,4},{33,6},{34,12},{35,14},{64,16},{65... | collective-permute-start | bytes 776 | tf_op jit(solution)/shard_map/ppermute | solution.py:267
  26.5 1.4 dynamic_slice.6
  29.3 6.4 %collective-permute-done = s32[2,32]{1,0:T(2,128)S(1)} collective-permute-done((s32[2,32]{1,0:T(2,128)S(1)}, s32[2,32]{1,0:T(2,128)S(1)}, u32[]{:S(2)}, u32[]{:S(2)}) %collective-permute-start) | collective-permute-done | bytes 288 | tf_op jit(solution)/shard_map/ppermute | solution.py:267
  36.4 1.0 all-to-all-done
  37.4 0.8 pick_roots.1
  38.2 1.3 copy-done.1
  39.6 4.6 %all-to-all-start.1 = ((bf16[8,2,256,256]{3,2,1,0:T(8,128)(2,1)}), bf16[8,2,256,256]{3,2,1,0:T(8,128)(2,1)S(1)}, u32[]{:S(2)}, u32[]{:S(2)}) async-start(bf16[8,2,256,256]{3,2,1,0:T(8,128)(2,1)} %copy-done.1), calls=%async_computation.2 | async-start | bytes 4194304 | tf_op jit(solution)/shard_map/all_to_all | solution.py:286
  44.2 26.8 %all-to-all-done.1.source = bf16[8,2,256,256]{3,2,1,0:T(8,128)(2,1)S(1)} async-done(((bf16[8,2,256,256]{3,2,1,0:T(8,128)(2,1)}), bf16[8,2,256,256]{3,2,1,0:T(8,128)(2,1)S(1)}, u32[]{:S(2)}, u32[]{:S(2)}) %all-to-all-start.1) | async-done | bytes 2097184 | tf_op jit(solution)/shard_map/all_to_all | solution.py:286
  71.0 1.6 hold_roots.1
  72.5 5.3 %collective-permute-start.1 = (bf16[4,2,256,256]{3,2,1,0:T(8,128)(2,1)}, bf16[4,2,256,256]{3,2,1,0:T(8,128)(2,1)S(1)}, u32[]{:S(2)}, u32[]{:S(2)}) collective-permute-start(bf16[4,2,256,256]{3,2,1,0:T(8,128)(2,1)} %hold_roots.1), channel_id=1, source_target_pairs={{0,64},{2,1},{8,2},{10,67},{4,0},{6,65},{12,66},{14,131},{16,96},{... | collective-permute-start | bytes 3145736 | tf_op jit(solution)/shard_map/ppermute | solution.py:296
  77.9 1.0 copy-done.6
  78.9 1.0 prepare.1
  79.9 21.8 %collective-permute-done.1.roots = bf16[4,2,256,256]{3,2,1,0:T(8,128)(2,1)S(1)} collective-permute-done((bf16[4,2,256,256]{3,2,1,0:T(8,128)(2,1)}, bf16[4,2,256,256]{3,2,1,0:T(8,128)(2,1)S(1)}, u32[]{:S(2)}, u32[]{:S(2)}) %collective-permute-start.1) | collective-permute-done | bytes 1048608 | tf_op jit(solution)/shard_map/ppermute | solution.py:296
  101.7 2.5 %precondition.1 = bf16[4,256,256]{2,1,0:T(8,128)(2,1)} custom-call(f32[4]{0:T(128)S(1)} %get-tuple-element.7.sizes, bf16[4,256,256]{2,1,0:T(8,128)(2,1)S(1)} %get-tuple-element.8.means, bf16[4,2,256,256]{3,2,1,0:T(8,128)(2,1)S(1)} %collective-permute-done.1.roots), custom_call_target="tpu_custom_call" | custom-call | flops 402653184 | bytes 2097152 | tf_op jit(solution)/shard_map/precondition/pallas_call | solution.py:206
  104.2 63.3 %all-gather.2.cloned.1.call-done.blocks = bf16[32,256,256]{2,1,0:T(8,128)(2,1)} async-done(((bf16[4,256,256]{2,1,0:T(8,128)(2,1)}), bf16[32,256,256]{2,1,0:T(8,128)(2,1)}) %all-gather.2.cloned.1.call-update) | async-done | bytes 4194320 | tf_op jit(solution)/shard_map/all_gather | solution.py:299
  167.5 2.2 %copy-done.3 = bf16[32,256,256]{2,1,0:T(8,128)(2,1)S(1)} copy-done((bf16[32,256,256]{2,1,0:T(8,128)(2,1)S(1)}, bf16[32,256,256]{2,1,0:T(8,128)(2,1)}, u32[]{:S(2)}) %copy-start.3) | copy-done | bytes 4194328
  169.7 2.8 %spread.1 = bf16[256,8192]{1,0:T(8,128)(2,1)} custom-call(s32[32]{0:T(128)S(1)} %fusion.8.index, bf16[32,256,256]{2,1,0:T(8,128)(2,1)S(1)} %copy-done.3), custom_call_target="tpu_custom_call" | custom-call | tf_op jit(solution)/shard_map/spread/pallas_call | solution.py:128
  (30 shorter events, 3.2 us)
Async XLA Ops:
  6.5 71.3 %reduce-scatter.2.cloned.1.call-start = ((), (), s32[]{:S(2)}) async-start(), calls=%async_computation.3 | async-start | bytes 4718592 | tf_op jit(solution)/shard_map/reduce_scatter | solution.py:265
  7.4 1.6 copy-start.4
  9.0 1.6 copy-start.5
  10.6 2.9 %copy-start.2 = (bf16[1,256,8192]{2,1,0:T(8,128)(2,1)S(1)}, bf16[1,256,8192]{2,1,0:T(8,128)(2,1)}, u32[]{:S(2)}) copy-start(bf16[1,256,8192]{2,1,0:T(8,128)(2,1)} %param.5) | copy-start | bytes 12582916
  15.1 2.0 %copy-start = (bf16[32,256,256]{2,1,0:T(8,128)(2,1)}, bf16[32,256,256]{2,1,0:T(8,128)(2,1)S(1)}, u32[]{:S(2)}) copy-start(bf16[32,256,256]{2,1,0:T(8,128)(2,1)S(1)} %place.1) | copy-start | bytes 12582916
  17.2 5.8 %copy-start.7 = (s32[1,32,1]{1,2,0:T(1,128)S(1)}, s32[1,32,1]{1,2,0:T(1,128)}, u32[]{:S(2)}) copy-start(s32[1,32,1]{1,2,0:T(1,128)} %param.6) | copy-start | bytes 388
  17.2 20.3 %all-to-all-start = ((bf16[4,2,2,256,256]{4,3,2,1,0:T(8,128)(2,1)}), bf16[4,2,2,256,256]{4,3,2,1,0:T(8,128)(2,1)S(1)}, u32[]{:S(2)}, u32[]{:S(2)}) async-start(bf16[4,2,2,256,256]{4,3,2,1,0:T(8,128)(2,1)} %bitcast.10), calls=%async_computation.1 | async-start | bytes 4194304 | tf_op jit(solution)/shard_map/all_to_all | solution.py:256
  23.0 12.7 %collective-permute-start = (s32[2,32]{1,0:T(2,128)S(1)}, s32[2,32]{1,0:T(2,128)S(1)}, u32[]{:S(2)}, u32[]{:S(2)}) collective-permute-start(s32[2,32]{1,0:T(2,128)S(1)} %pad_add_fusion), channel_id=1, source_target_pairs={{0,0},{1,2},{2,8},{3,10},{32,4},{33,6},{34,12},{35,14},{64,16},{65... | collective-permute-start | bytes 776 | tf_op jit(solution)/shard_map/ppermute | solution.py:267
  38.2 1.4 copy-start.1
  39.6 31.4 %all-to-all-start.1 = ((bf16[8,2,256,256]{3,2,1,0:T(8,128)(2,1)}), bf16[8,2,256,256]{3,2,1,0:T(8,128)(2,1)S(1)}, u32[]{:S(2)}, u32[]{:S(2)}) async-start(bf16[8,2,256,256]{3,2,1,0:T(8,128)(2,1)} %copy-done.1), calls=%async_computation.2 | async-start | bytes 4194304 | tf_op jit(solution)/shard_map/all_to_all | solution.py:286
  44.2 123.4 %all-gather.2.cloned.1.call-start = ((), (), s32[]{:S(2)}) async-start(), calls=%async_computation.4 | async-start | bytes 4718592 | tf_op jit(solution)/shard_map/all_gather | solution.py:299
  72.5 29.1 %collective-permute-start.1 = (bf16[4,2,256,256]{3,2,1,0:T(8,128)(2,1)}, bf16[4,2,256,256]{3,2,1,0:T(8,128)(2,1)S(1)}, u32[]{:S(2)}, u32[]{:S(2)}) collective-permute-start(bf16[4,2,256,256]{3,2,1,0:T(8,128)(2,1)} %hold_roots.1), channel_id=1, source_target_pairs={{0,64},{2,1},{8,2},{10,67},{4,0},{6,65},{12,66},{14,131},{16,96},{... | collective-permute-start | bytes 3145736 | tf_op jit(solution)/shard_map/ppermute | solution.py:296
  77.9 1.0 copy-start.6
  167.5 2.2 %copy-start.3 = (bf16[32,256,256]{2,1,0:T(8,128)(2,1)S(1)}, bf16[32,256,256]{2,1,0:T(8,128)(2,1)}, u32[]{:S(2)}) copy-start(bf16[32,256,256]{2,1,0:T(8,128)(2,1)} %all-gather.2.cloned.1.call-done.blocks) | copy-start | bytes 12582916
Sparse Core Ops, SparseCore 0:
  17.3 58.1 reduce-scatter.1
  104.4 63.1 all-gather.1
